TPU v7x, 32 devices: a whole 2x2x4 slice. The times are simulated.
32 devices in a mesh: dp: 8 (over y, x, core), seq: 4 (over z).
Axes of the slice: x: 2, y: 2, z: 4, core: 2. Of those that a mesh axis runs over, the one named last changes fastest.
Arguments:
- tokens: bfloat16 [8, 1024, 1024], P('dp', 'seq'), may hold values from -6 to 6
- first_values: bfloat16 [8, 1024, 1024], P('dp', 'seq'), may hold values from -6 to 6
- out_grad: bfloat16 [8, 1024, 1024], P('dp', 'seq'), may hold values from -6 to 6
- segments: int32 [8, 1024], P('dp', 'seq'), may hold values from 0 to 3, as said below
- span_order: int32 [4], replicated, may hold values from 0 to 3, as said below
- qkv_weight: float32 [1024, 3072], P('dp'), may hold values from -0.1875 to 0.1875
- out_weight: float32 [1024, 1024], P('dp'), may hold values from -1 to 1
- gate_up_weight: float32 [1024, 5632], P('dp'), may hold values from -0.1875 to 0.1875
- down_weight: float32 [2816, 1024], P('dp'), may hold values from -0.109375 to 0.109375
- norm_gains: float32 [1024, 2], P('dp'), may hold values from 0.5 to 1.5
- first_qkv: float32 [1024, 3072], P('dp'), may hold values from -256 to 256
- first_out: float32 [1024, 1024], P('dp'), may hold values from -56 to 56
- first_gate_up: float32 [1024, 5632], P('dp'), may hold values from -192 to 192
- first_down: float32 [2816, 1024], P('dp'), may hold values from -256 to 256
- first_gains: float32 [1024, 2], P('dp'), may hold values from -512 to 512
- second_qkv: float32 [1024, 3072], P('dp'), may hold values from 2048 to 8192
- second_out: float32 [1024, 1024], P('dp'), may hold values from 81.92 to 327.68
- second_gate_up: float32 [1024, 5632], P('dp'), may hold values from 1003.52 to 4014.08
- second_down: float32 [2816, 1024], P('dp'), may hold values from 2048 to 8192
- second_gains: float32 [1024, 2], P('dp'), may hold values from 8192 to 32768
Outputs:
- layer_out: bfloat16 [8, 1024, 1024], P('dp', 'seq')
- tokens_grad: float32 [8, 1024, 1024], P('dp', 'seq')
- values_grad: float32 [8, 1024, 1024], P('dp', 'seq')
- new_qkv: float32 [1024, 3072], P('dp')
- new_out: float32 [1024, 1024], P('dp')
- new_gate_up: float32 [1024, 5632], P('dp')
- new_down: float32 [2816, 1024], P('dp')
- new_gains: float32 [1024, 2], P('dp')
- next_first_qkv: float32 [1024, 3072], P('dp')
- next_first_out: float32 [1024, 1024], P('dp')
- next_first_gate_up: float32 [1024, 5632], P('dp')
- next_first_down: float32 [2816, 1024], P('dp')
- next_first_gains: float32 [1024, 2], P('dp')
- next_second_qkv: float32 [1024, 3072], P('dp')
- next_second_out: float32 [1024, 1024], P('dp')
- next_second_gate_up: float32 [1024, 5632], P('dp')
- next_second_down: float32 [2816, 1024], P('dp')
- next_second_gains: float32 [1024, 2], P('dp')
Inputs may be any that keep to these rules, and one draw needn't show every extreme that they name: `segments`: read in order of positions, a sequence's ids never fall; every sequence has ids 0 to 3, and id 2 begins within the first 256 positions and ends within the last 256. `span_order`: A permutation of the span numbers.
All inputs are finite; a program needn't handle non-finite values.
Results may differ from a plain program's by a relative error of at most 0.015.
The roundings to bfloat16 on the way count: a program that leaves them out, or rounds other values in their place, can miss the bound.
Values may be sent and summed in bfloat16 or wider, within the bound.
A program may use at most 320 MiB of HBM per device.

v0:
```python
import functools
import math

import jax
import jax.numpy as jnp
from jax import lax
from jax.experimental import pallas as pl
from jax.experimental.pallas import tpu as pltpu
from jax.sharding import PartitionSpec as P

HEAD_DIM = 64
STEP = 10


NORM_EPS = 1e-06
ADAM_EPS = 1e-08
BLEND_MIX = 0.5
BETA_FIRST = 0.5
BETA_SECOND = 0.5
MATRIX_RATE = 0.06
MATRIX_DECAY = 0.1
GAIN_RATE = 0.5
ROPE_BASE = 10000.0
MASK_FILL = -1e30
SCALE = HEAD_DIM ** (-0.5)

BF = jnp.bfloat16
F32 = jnp.float32


def dot_nn(left, right):
    return lax.dot_general(left, right, (((1,), (0,)), ((), ())), preferred_element_type=F32)


def dot_nt(left, right):
    return lax.dot_general(left, right, (((1,), (1,)), ((), ())), preferred_element_type=F32)


def dot_tn(left, right):
    return lax.dot_general(left, right, (((0,), (0,)), ((), ())), preferred_element_type=F32)


def normalize_parts(matrix):
    inverse = lax.rsqrt(jnp.mean(matrix * matrix, axis=-1, keepdims=True) + NORM_EPS)
    return (matrix * inverse, inverse)


def norm_backward(grad_rows, scaled, inverse, gain_column):
    pushed = grad_rows * gain_column
    return inverse * (pushed - scaled * jnp.mean(pushed * scaled, axis=-1, keepdims=True))


def rotary(positions):
    half_width = HEAD_DIM // 2
    frequency = jnp.exp(
        jnp.arange(half_width, dtype=F32) * (-math.log(ROPE_BASE) / half_width)
    )
    angles = positions.astype(F32)[:, None] * frequency[None, :]
    return (jnp.cos(angles)[:, None, :], jnp.sin(angles)[:, None, :])


def rotate(head_rows, cosine, sine_table):
    half_width = head_rows.shape[-1] // 2
    lower_half = head_rows[..., :half_width]
    upper_half = head_rows[..., half_width:]
    return jnp.concatenate(
        [
            lower_half * cosine - upper_half * sine_table,
            upper_half * cosine + lower_half * sine_table,
        ],
        axis=-1,
    )


def apply_adamw(master, first_state, second_state, gradient, rate, decay):
    next_first = BETA_FIRST * first_state + (1.0 - BETA_FIRST) * gradient
    next_second = BETA_SECOND * second_state + (1.0 - BETA_SECOND) * gradient * gradient
    first_hat = next_first / (1.0 - BETA_FIRST**STEP)
    second_hat = next_second / (1.0 - BETA_SECOND**STEP)
    new_master = master - rate * (first_hat / (jnp.sqrt(second_hat) + ADAM_EPS) + decay * master)
    return (new_master, next_first, next_second)


MESH = pl.DeviceIdType.MESH
VMEM_BYTES = 58 << 20


def full_spec():
    return pl.BlockSpec(memory_space=pltpu.VMEM)


def any_spec():
    return pl.BlockSpec(memory_space=pl.ANY)


class Place:
    def __init__(self, dp_count, span_count):
        self.dp_count = dp_count
        self.span_count = span_count
        self.inner_count = dp_count // 4
        self.dp = lax.axis_index("dp")
        self.span = lax.axis_index("seq")
        self.core = lax.rem(self.dp, 2)
        self.inner = lax.rem(self.dp // 2, self.inner_count)
        self.outer = self.dp // (2 * self.inner_count)

    def at(self, outer, inner, core):
        return (outer * self.inner_count + inner) * 2 + core

    def inner_plus(self, offset):
        return lax.rem(self.inner + offset, self.inner_count)

    def greet_all(self):
        barrier = pltpu.get_barrier_semaphore()
        for offset in range(1, self.dp_count):
            pl.semaphore_signal(
                barrier,
                inc=1,
                device_id=(lax.rem(self.dp + offset, self.dp_count), self.span),
                device_id_type=MESH,
            )
        for offset in range(1, self.span_count):
            pl.semaphore_signal(
                barrier,
                inc=1,
                device_id=(self.dp, lax.rem(self.span + offset, self.span_count)),
                device_id_type=MESH,
            )
        pl.semaphore_wait(barrier, self.dp_count + self.span_count - 2)


def remote(source, target, send_sem, recv_sem, device):
    return pltpu.make_async_remote_copy(
        src_ref=source,
        dst_ref=target,
        send_sem=send_sem,
        recv_sem=recv_sem,
        device_id=device,
        device_id_type=MESH,
    )


def half_rows(rows):
    return rows // 2 // 16 * 16


class Gather:
    def __init__(self, place, whole, columns, send_sems, recv_sems):
        self.place = place
        self.whole = whole
        self.columns = columns
        self.rows = whole.shape[0] // place.dp_count
        self.send_sems = send_sems
        self.recv_sems = recv_sems
        count = place.inner_count
        self.near, self.lower, self.upper, self.pair = 0, count, 2 * count, 3 * count

    @staticmethod
    def slots(inner_count):
        return 6 * inner_count + 1

    def block(self, index, part=None):
        first = half_rows(self.rows)
        start, size = {None: (0, self.rows), 0: (0, first), 1: (first, self.rows - first)}[part]
        return self.whole.at[
            pl.ds(pl.multiple_of(index * self.rows + start, 16), size), self.columns
        ]

    def send(self, source, target, slot, far_slot, device):
        remote(
            source, target, self.send_sems.at[slot], self.recv_sems.at[far_slot], (device, self.place.span)
        ).start()

    def left(self, block, slot):
        remote(
            block, block, self.send_sems.at[slot], self.recv_sems.at[slot], (self.place.dp, self.place.span)
        ).wait_send()

    def arrived(self, block, slot):
        remote(
            block, block, self.send_sems.at[slot], self.recv_sems.at[slot], (self.place.dp, self.place.span)
        ).wait_recv()

    def sibling(self, block, slot):
        place = self.place
        self.send(block, block, slot, slot, place.at(place.outer, place.inner, 1 - place.core))

    def begin(self):
        place, count = self.place, self.place.inner_count
        mine = self.block(place.dp)
        self.send(mine, mine, 0, 0, place.at(1 - place.outer, place.inner, place.core))
        for offset in range(1, count):
            self.send(
                mine,
                mine,
                offset,
                count - offset,
                place.at(place.outer, place.inner_plus(offset), place.core),
            )
        self.sibling(mine, self.pair)

    def forward(self):
        place, count = self.place, self.place.inner_count
        across = place.at(1 - place.outer, place.inner, place.core)
        self.arrived(self.block(across), 0)
        for offset in range(1, count):
            self.send(
                self.block(across, 0),
                self.block(across, 0),
                self.lower + offset,
                self.lower + count - offset,
                place.at(place.outer, place.inner_plus(offset), place.core),
            )
        for offset in range(1, count):
            beside = place.at(place.outer, place.inner_plus(offset), place.core)
            self.arrived(self.block(beside), offset)
            self.send(
                self.block(beside, 1),
                self.block(beside, 1),
                self.upper + offset,
                self.upper + offset,
                across,
            )
        self.sibling(self.block(across), self.pair + count)
        for offset in range(1, count):
            beside = place.at(place.outer, place.inner_plus(offset), place.core)
            self.sibling(self.block(beside), self.pair + offset)

    def share(self):
        place, count = self.place, self.place.inner_count
        for offset in range(1, count):
            far = place.at(1 - place.outer, place.inner_plus(offset), place.core)
            self.arrived(self.block(far, 0), self.lower + offset)
            self.sibling(self.block(far, 0), self.pair + count + offset)
            self.arrived(self.block(far, 1), self.upper + offset)
            self.sibling(self.block(far, 1), self.pair + 2 * count + offset)

    def end(self):
        place, count = self.place, self.place.inner_count
        other = 1 - place.core
        self.arrived(self.block(place.at(place.outer, place.inner, other)), self.pair)
        self.arrived(self.block(place.at(1 - place.outer, place.inner, other)), self.pair + count)
        for offset in range(1, count):
            inner = place.inner_plus(offset)
            self.arrived(self.block(place.at(place.outer, inner, other)), self.pair + offset)
            far = place.at(1 - place.outer, inner, other)
            self.arrived(self.block(far, 0), self.pair + count + offset)
            self.arrived(self.block(far, 1), self.pair + 2 * count + offset)
        mine = self.block(place.dp)
        across = self.block(place.at(1 - place.outer, place.inner, place.core))
        self.left(mine, 0)
        self.left(mine, self.pair)
        self.left(across, self.pair + count)
        for offset in range(1, count):
            inner = place.inner_plus(offset)
            beside = place.at(place.outer, inner, place.core)
            far = place.at(1 - place.outer, inner, place.core)
            self.left(mine, offset)
            self.left(self.block(beside), self.pair + offset)
            self.left(
                self.block(place.at(1 - place.outer, place.inner, place.core), 0),
                self.lower + offset,
            )
            self.left(self.block(beside, 1), self.upper + offset)
            self.left(self.block(far, 0), self.pair + count + offset)
            self.left(self.block(far, 1), self.pair + 2 * count + offset)


class Exchange:
    def __init__(self, place, sources, targets, send_sems, recv_sems):
        self.place = place
        self.sources = sources
        self.targets = targets
        self.send_sems = send_sems
        self.recv_sems = recv_sems

    def copy(self, offset):
        place = self.place
        count = place.span_count
        peer = lax.rem(place.span + offset, count)
        return remote(
            self.sources.at[peer],
            self.targets.at[place.span],
            self.send_sems.at[offset],
            self.recv_sems.at[count - offset],
            (place.dp, peer),
        )

    def start(self):
        for offset in range(1, self.place.span_count):
            self.copy(offset).start()
        self.targets[self.place.span] = self.sources[self.place.span]

    def wait(self):
        place = self.place
        count = place.span_count
        for offset in range(1, count):
            peer = lax.rem(place.span + offset, count)
            remote(
                self.sources.at[peer],
                self.targets.at[peer],
                self.send_sems.at[offset],
                self.recv_sems.at[offset],
                (place.dp, peer),
            ).wait_recv()

    def finish(self):
        for offset in range(1, self.place.span_count):
            self.copy(offset).wait_send()


def cast_rows(source, target, first, moves=None):
    rows = source.shape[0]

    def step(index, unused):
        at = pl.ds(pl.multiple_of(index * 16, 16), 16)
        there = pl.ds(pl.multiple_of(first + index * 16, 16), 16)
        for from_columns, to_columns in moves or ((slice(None), slice(None)),):
            target[there, to_columns] = source[at, from_columns].astype(BF)
        return unused

    lax.fori_loop(0, rows // 16, step, 0)


def swap_halves(rows):
    width = rows.shape[1]
    half = HEAD_DIM // 2
    if width % 128:
        pieces = []
        for start in range(0, width, HEAD_DIM):
            pieces += [rows[:, start + half : start + HEAD_DIM], rows[:, start : start + half]]
        return jnp.concatenate(pieces, axis=1)
    lane = lax.broadcasted_iota(jnp.int32, rows.shape, 1)
    return jnp.where(
        lane % HEAD_DIM < half, pltpu.roll(rows, width - half, 1), pltpu.roll(rows, half, 1)
    )


def angles_of(cosine, sine, position, heads):
    half = HEAD_DIM // 2
    back = lax.rem(cosine.shape[1] - half * position, cosine.shape[1])
    cos_half = pltpu.roll(cosine[...], back, 1)[:, :half]
    sin_half = pltpu.roll(sine[...], back, 1)[:, :half]
    return (
        jnp.concatenate([cos_half] * (2 * heads), axis=1),
        jnp.concatenate([-sin_half, sin_half] * heads, axis=1),
    )


def slot_with(order, position):
    slot = 0
    for index in range(order.shape[0]):
        slot = jnp.where(order[index] == position, index, slot)
    return slot


def segment_starts(bounds, rows, first):
    position = lax.broadcasted_iota(jnp.int32, (rows, 1), 0) + first
    position = position.astype(F32)
    start = jnp.zeros((rows, 1), F32)
    for cut in bounds:
        start = jnp.where(position >= cut, cut, start)
    return position, start


def head_part(matrix, head):
    if matrix.shape[1] == HEAD_DIM:
        return matrix
    lane = lax.broadcasted_iota(jnp.int32, (1, matrix.shape[1]), 1)
    return jnp.where(lane // HEAD_DIM == head, matrix, jnp.zeros_like(matrix))


def forward_kernel(
    dp_count,
    span_count,
    order,
    tokens,
    first_values,
    segments,
    gains_mine,
    qkv_mine,
    out_mine,
    gate_up_mine,
    down_mine,
    cosine,
    sine,
    out_grad,
    counts_out,
    gains_out,
    layer_low,
    mid_grad,
    mid_grad_low,
    normed_left,
    attended_left,
    attended_grad,
    qkv_result,
    normed_result,
    query_result,
    key_result,
    value_result,
    raw_result,
    lse_result,
    gate_up_grad_result,
    activation_result,
    normed_out,
    query_out,
    key_out,
    value_out,
    raw_out,
    lse_out,
    gate_up_grad,
    activation_left,
    gains_send,
    qkv_held,
    out_whole,
    gate_up_whole,
    down_whole,
    qkv_whole,
    attended,
    normed,
    outward,
    normed_grad,
    gains_all,
    counts_send,
    counts_all,
    first_send,
    first_all,
    normed_all,
    scores_kept,
    attended_send,
    attended_all,
    gather_send,
    gather_recv,
    gains_send_sem,
    gains_recv_sem,
    counts_send_sem,
    counts_recv_sem,
    first_send_sem,
    first_recv_sem,
    ring_send,
    ring_recv,
    attended_send_sem,
    attended_recv_sem,
    local_sem,
    result_sem,
):
    place = Place(dp_count, span_count)
    rows, width = tokens.shape
    group = width // span_count
    hidden = down_whole.shape[0]
    owned = out_mine.shape[0]
    heads = group // HEAD_DIM
    last = span_count - 1
    span = place.span

    qkv_loads = []
    for part in range(3):
        first = pl.multiple_of(part * width + span * group, 128)
        copy = pltpu.make_async_copy(
            qkv_mine.at[:, pl.ds(first, group)],
            qkv_held.at[:, part * group : (part + 1) * group],
            local_sem.at[part],
        )
        copy.start()
        qkv_loads.append(copy)

    place.greet_all()
    gains_send[...] = jnp.zeros_like(gains_send)
    gains_send[0:2, :] = gains_mine[...].astype(BF).astype(F32)
    gains_all[place.dp] = gains_send[...]
    gains_copies = []
    for offset in range(1, dp_count):
        peer = lax.rem(place.dp + offset, dp_count)
        copy = remote(
            gains_send,
            gains_all.at[place.dp],
            gains_send_sem.at[offset],
            gains_recv_sem.at[dp_count - offset],
            (peer, span),
        )
        copy.start()
        gains_copies.append(copy)
    parts = hidden_parts(hidden)
    moves = []
    gate_up_columns = []
    for start, size in parts:
        moves.append((slice(start, start + size), slice(2 * start, 2 * start + size)))
        moves.append(
            (
                slice(hidden + start, hidden + start + size),
                slice(2 * start + size, 2 * start + 2 * size),
            )
        )
        gate_up_columns.append(slice(2 * start, 2 * (start + size)))
    every = slice(None)
    sources = [(qkv_whole, every), (out_whole, every), (down_whole, every)]
    sources += [(gate_up_whole, columns) for columns in gate_up_columns]
    gathers = [
        Gather(place, whole, columns, gather_send.at[i], gather_recv.at[i])
        for i, (whole, columns) in enumerate(sources)
    ]
    qkv_gather, out_gather, down_gather = gathers[:3]
    gate_up_gathers = gathers[3:]
    for copy in qkv_loads:
        copy.wait()
    cast_rows(qkv_held, qkv_whole, place.dp * owned)
    qkv_gather.begin()
    for index in range(span_count):
        first_send[index] = first_values[:, index * group : (index + 1) * group]
    first_exchange = Exchange(place, first_send, first_all, first_send_sem, first_recv_sem)
    ids = segments[...]
    row = lax.broadcasted_iota(jnp.int32, (8, 128), 0)
    counts = jnp.zeros((8, 128), F32)
    for cut in range(3):
        below = jnp.sum(jnp.where(ids <= cut, 1.0, 0.0), axis=1, keepdims=True)
        counts = jnp.where(row == cut, below, counts)
    for index in range(span_count):
        counts_send[index] = counts
    counts_exchange = Exchange(place, counts_send, counts_all, counts_send_sem, counts_recv_sem)
    counts_exchange.start()

    residual = tokens[...].astype(F32)
    scaled = residual * lax.rsqrt(jnp.mean(residual * residual, axis=1, keepdims=True) + NORM_EPS)
    for offset in range(1, dp_count):
        peer = lax.rem(place.dp + offset, dp_count)
        remote(
            gains_send,
            gains_all.at[peer],
            gains_send_sem.at[offset],
            gains_recv_sem.at[offset],
            (peer, span),
        ).wait_recv()
    gains_row = jnp.concatenate([gains_all[i] for i in range(dp_count)], axis=1)
    gains_out[...] = gains_row
    normed_all[span] = (scaled * gains_row[0:1, :]).astype(BF)

    def pass_on(block, step, way):
        return remote(
            normed_all.at[block],
            normed_all.at[block],
            ring_send.at[way, step],
            ring_recv.at[way, step],
            (place.dp, jnp.where(way == 0, jnp.minimum(span + 1, last), jnp.maximum(span - 1, 0))),
        )

    @pl.when(span < last)
    def up():
        pass_on(span, 0, 0).start()

    @pl.when(span > 0)
    def down():
        pass_on(span, 0, 1).start()

    cast_rows(out_mine, out_whole, place.dp * owned)
    out_gather.begin()
    cast_rows(down_mine, down_whole, place.dp * down_mine.shape[0])
    qkv_gather.forward()
    down_gather.begin()
    cast_rows(gate_up_mine, gate_up_whole, place.dp * owned, moves)
    for member in gate_up_gathers:
        member.begin()
    qkv_gather.share()
    out_gather.forward()

    for step in range(1, span_count):

        @pl.when(span - step >= 0)
        def from_below():
            block = jnp.maximum(span - step, 0)
            pass_on(block, step - 1, 0).wait_recv()

            @pl.when(span < last)
            def on():
                pass_on(block, step, 0).start()

        @pl.when(span + step <= last)
        def from_above():
            block = jnp.minimum(span + step, last)
            pass_on(block, step - 1, 1).wait_recv()

            @pl.when(span > 0)
            def on():
                pass_on(block, step, 1).start()

        if step == last - 1:
            first_exchange.start()

    qkv_gather.end()
    results = []

    def keep(source, target):
        copy = pltpu.make_async_copy(source, target, result_sem.at[len(results)])
        copy.start()
        results.append(copy)

    keep(qkv_whole, qkv_result)
    counts_exchange.wait()
    cuts = counts_all[0]
    for index in range(1, span_count):
        cuts = cuts + counts_all[index]
    counts_out[...] = cuts
    bounds = [cuts[i : i + 1, 0:1] for i in range(3)]

    def project(position, unused):
        slot = slot_with(order, position)
        normed_here = normed_all[slot]
        normed_out[:, pl.ds(pl.multiple_of(position * rows, rows), rows)] = jnp.transpose(normed_here)
        mixed = dot_nn(normed_here, qkv_whole[...])
        cos_here, sin_here = angles_of(cosine, sine, position, heads)
        query = mixed[:, :group]
        key = mixed[:, group : 2 * group]
        query_out[position] = (query * cos_here + swap_halves(query) * sin_here).astype(BF)
        key_out[position] = (key * cos_here + swap_halves(key) * sin_here).astype(BF)
        raw_out[position] = BLEND_MIX * mixed[:, 2 * group :]
        return unused

    def blend(position, unused):
        slot = slot_with(order, position)
        value_out[position] = (
            raw_out[position] + (1.0 - BLEND_MIX) * first_all[slot].astype(F32)
        ).astype(BF)
        return unused

    lax.fori_loop(0, span_count, project, 0)
    first_exchange.wait()
    lax.fori_loop(0, span_count, blend, 0)
    for source, target in (
        (normed_out, normed_result),
        (query_out, query_result),
        (key_out, key_result),
        (value_out, value_result),
    ):
        keep(source, target)
    out_gather.share()
    down_gather.forward()

    def attend(position, unused):
        query = query_out[position]
        parts = [head_part(query, head) for head in range(heads)]
        query_position, start = segment_starts(bounds, rows, position * rows)

        def score(other, highest):
            key = key_out[other]
            key_position = (
                lax.broadcasted_iota(jnp.int32, (1, rows), 1) + other * rows
            ).astype(F32)
            allowed = (key_position <= query_position) & (key_position >= start)
            found = []
            for head in range(heads):
                masked = jnp.where(allowed, dot_nt(parts[head], key) * SCALE, MASK_FILL)
                scores_kept[head, other] = masked
                found.append(jnp.maximum(highest[head], jnp.max(masked, axis=1, keepdims=True)))
            return tuple(found)

        highest = lax.fori_loop(
            0, position + 1, score, (jnp.full((rows, 1), MASK_FILL, F32),) * heads
        )

        def raise_scores(other, total):
            added = []
            for head in range(heads):
                raised = jnp.exp(scores_kept[head, other] - highest[head])
                scores_kept[head, other] = raised
                added.append(total[head] + jnp.sum(raised, axis=1, keepdims=True))
            return tuple(added)

        total = lax.fori_loop(
            0, position + 1, raise_scores, (jnp.zeros((rows, 1), F32),) * heads
        )
        inverse = [1.0 / member for member in total]

        def gather_values(other, attended):
            value = value_out[other]
            for head in range(heads):
                weights = (scores_kept[head, other] * inverse[head]).astype(BF)
                attended = attended + dot_nn(weights, head_part(value, head))
            return attended

        raw_out[position] = lax.fori_loop(
            0, position + 1, gather_values, jnp.zeros((rows, group), F32)
        )
        lane = lax.broadcasted_iota(jnp.int32, (rows, 128), 1)
        kept = jnp.zeros((rows, 128), F32)
        for head in range(heads):
            kept = jnp.where(lane == head, highest[head] + jnp.log(total[head]), kept)
        lse_out[position] = kept

        @pl.when(position == span_count // 2 - 1)
        def second_parts():
            for member in gate_up_gathers[1:-1]:
                member.forward()

        @pl.when(position == span_count - 2)
        def last_part():
            gate_up_gathers[-1].forward()

        return unused

    gate_up_gathers[0].forward()
    lax.fori_loop(0, span_count, attend, 0)
    down_gather.share()

    for index in range(span_count):
        attended_send[index] = raw_out[order[index]].astype(BF)
    attended_exchange = Exchange(
        place, attended_send, attended_all, attended_send_sem, attended_recv_sem
    )
    attended_exchange.start()
    keep(raw_out, raw_result)
    keep(lse_out, lse_result)
    gate_up_gathers[0].share()
    out_gather.end()
    attended_exchange.wait()
    attended[...] = jnp.concatenate([attended_all[i] for i in range(span_count)], axis=1)

    hidden_mid = tokens[...].astype(F32) + dot_nn(attended[...], out_whole[...])
    outward[...] = hidden_mid
    scaled, inverse = normalize_parts(hidden_mid)
    normed[...] = (scaled * gains_out[1:2, :]).astype(BF)
    normed_left[...] = jnp.transpose(normed[...])
    attended_left[...] = jnp.transpose(attended[...])
    normed_grad[...] = jnp.zeros_like(normed_grad)
    down_gather.end()
    block = 256

    per_part = parts[0][1] // block

    def step(index, unused):
        for number in range(len(parts)):

            @pl.when(index == number * per_part)
            def columns_here():
                if number + 1 < len(parts):
                    gate_up_gathers[number + 1].share()
                gate_up_gathers[number].end()

        start = index // per_part * per_part * block
        size = jnp.minimum(per_part * block, hidden - start)
        offset = lax.rem(index, per_part) * block
        gate_at = pl.ds(pl.multiple_of(2 * start + offset, block), block)
        up_at = pl.ds(pl.multiple_of(2 * start + size + offset, block), block)
        here = pl.ds(pl.multiple_of(index * block, block), block)
        there = pl.ds(pl.multiple_of(hidden + index * block, block), block)
        gate = dot_nn(normed[...], gate_up_whole[:, gate_at])
        upward = dot_nn(normed[...], gate_up_whole[:, up_at])
        activation_grad = dot_nt(out_grad[...], down_whole[here, :])
        sigmoid = jax.nn.sigmoid(gate)
        swish = gate * sigmoid
        activation = (swish * upward).astype(BF)
        activation_left[here, :] = jnp.transpose(activation)
        gate_grad = (
            activation_grad * upward * sigmoid * (1.0 + gate * (1.0 - sigmoid))
        ).astype(BF)
        up_grad = (activation_grad * swish).astype(BF)
        gate_up_grad[:, here] = gate_grad
        gate_up_grad[:, there] = up_grad
        outward[...] += dot_nn(activation, down_whole[here, :])
        normed_grad[...] += dot_nt(gate_grad, gate_up_whole[:, gate_at]) + dot_nt(
            up_grad, gate_up_whole[:, up_at]
        )
        return unused

    lax.fori_loop(0, hidden // block, step, 0)
    keep(gate_up_grad, gate_up_grad_result)
    keep(activation_left, activation_result)
    layer_low[...] = outward[...].astype(BF)
    hidden_mid = tokens[...].astype(F32) + dot_nn(attended[...], out_whole[...])
    scaled, inverse = normalize_parts(hidden_mid)
    grad = out_grad[...].astype(F32) + norm_backward(
        normed_grad[...], scaled, inverse, gains_out[1:2, :]
    )
    mid_grad[...] = grad
    mid_grad_low[...] = grad.astype(BF)
    attended_grad[...] = dot_nt(mid_grad_low[...], out_whole[...]).astype(BF)

    for copy in gains_copies:
        copy.wait_send()
    for exchange in (first_exchange, counts_exchange, attended_exchange):
        exchange.finish()
    for step in range(span_count):

        @pl.when((span - step >= 0) & (span < last))
        def sent_up():
            pass_on(jnp.maximum(span - step, 0), step, 0).wait_send()

        @pl.when((span + step <= last) & (span > 0))
        def sent_down():
            pass_on(jnp.minimum(span + step, last), step, 1).wait_send()

    for copy in results:
        copy.wait()


def hidden_parts(hidden):
    size = 256 * -(-hidden // 1024)
    return [(start, min(size, hidden - start)) for start in range(0, hidden, size)]


def forward_call(
    dp_count, span_count, order, tokens, first_values, segments, gains_mine, qkv_mine,
    out_mine, gate_up_mine, down_mine, cosine, sine, out_grad,
):
    rows, width = tokens.shape
    group = width // span_count
    heads = group // HEAD_DIM
    owned = qkv_mine.shape[0]
    doubled = gate_up_mine.shape[1]
    hidden = doubled // 2
    gathers = 3 + len(hidden_parts(hidden))
    slots = Gather.slots(dp_count // 4)
    dma = pltpu.SemaphoreType.DMA
    by_span = (span_count, rows, group)
    kept = (
        ((width, span_count * rows), BF),
        (by_span, BF),
        (by_span, BF),
        (by_span, BF),
        (by_span, F32),
        ((span_count, rows, 128), F32),
        ((rows, doubled), BF),
        ((hidden, rows), BF),
    )
    return pl.pallas_call(
        functools.partial(forward_kernel, dp_count, span_count),
        out_shape=(
            jax.ShapeDtypeStruct((8, 128), F32),
            jax.ShapeDtypeStruct((8, width), F32),
            jax.ShapeDtypeStruct((rows, width), BF),
            jax.ShapeDtypeStruct((rows, width), F32),
            jax.ShapeDtypeStruct((rows, width), BF),
            jax.ShapeDtypeStruct((width, rows), BF),
            jax.ShapeDtypeStruct((width, rows), BF),
            jax.ShapeDtypeStruct((rows, width), BF),
            jax.ShapeDtypeStruct((width, 3 * group), BF),
        )
        + tuple(jax.ShapeDtypeStruct(shape, kind) for shape, kind in kept),
        in_specs=[pl.BlockSpec(memory_space=pltpu.SMEM)]
        + [full_spec()] * 4
        + [any_spec()]
        + [full_spec()] * 6,
        out_specs=(full_spec(),) * 8 + (any_spec(),) * 9,
        scratch_shapes=[pltpu.VMEM(shape, kind) for shape, kind in kept]
        + [
            pltpu.VMEM((8, owned), F32),
            pltpu.VMEM((owned, 3 * group), F32),
            pltpu.VMEM((width, width), BF),
            pltpu.VMEM((width, doubled), BF),
            pltpu.VMEM((hidden, width), BF),
            pltpu.VMEM((width, 3 * group), BF),
            pltpu.VMEM((rows, width), BF),
            pltpu.VMEM((rows, width), BF),
            pltpu.VMEM((rows, width), F32),
            pltpu.VMEM((rows, width), F32),
            pltpu.VMEM((dp_count, 8, owned), F32),
            pltpu.VMEM((span_count, 8, 128), F32),
            pltpu.VMEM((span_count, 8, 128), F32),
            pltpu.VMEM(by_span, BF),
            pltpu.VMEM(by_span, BF),
            pltpu.VMEM((span_count, rows, width), BF),
            pltpu.VMEM((heads, span_count, rows, rows), F32),
            pltpu.VMEM(by_span, BF),
            pltpu.VMEM(by_span, BF),
            dma((gathers, slots)),
            dma((gathers, slots)),
            dma((dp_count,)),
            dma((dp_count,)),
            dma((span_count,)),
            dma((span_count,)),
            dma((span_count,)),
            dma((span_count,)),
            dma((2, span_count)),
            dma((2, span_count)),
            dma((span_count,)),
            dma((span_count,)),
            dma((3,)),
            dma((9,)),
        ],
        compiler_params=pltpu.CompilerParams(
            collective_id=0, has_side_effects=True, vmem_limit_bytes=61 << 20
        ),
    )(
        order, tokens, first_values, segments, gains_mine, qkv_mine, out_mine,
        gate_up_mine, down_mine, cosine, sine, out_grad,
    )


class Pair:
    def __init__(
        self,
        place,
        left_whole,
        left,
        left_other,
        right_whole,
        right,
        right_other,
        send_sems,
        recv_sems,
    ):
        self.place = place
        self.left = left
        self.left_other = left_other
        self.right = right
        self.right_other = right_other
        other = (place.at(place.outer, place.inner, 1 - place.core), place.span)
        self.left_copy = remote(
            left_whole.at[:, 1 - place.core], left_other, send_sems.at[0], recv_sems.at[0], other
        )
        self.own_copy = pltpu.make_async_copy(
            left_whole.at[:, place.core], left, send_sems.at[2]
        )
        self.right_copy = remote(
            right_whole, right_other, send_sems.at[1], recv_sems.at[1], other
        )
        self.own_right = None
        if right_whole is not right:
            self.own_right = pltpu.make_async_copy(right_whole, right, send_sems.at[3])

    def lend_left(self):
        self.left_copy.start()
        self.own_copy.start()

    def lend_right(self):
        self.right_copy.start()
        self.own_right.start()

    def wait(self):
        self.own_copy.wait()
        if self.own_right is not None:
            self.own_right.wait()
        self.left_copy.wait_recv()
        self.right_copy.wait_recv()

    def finish(self):
        self.left_copy.wait_send()
        self.right_copy.wait_send()

    def product(self, outer, inner, columns):
        chip = outer * self.place.inner_count + inner
        depth = self.right.shape[1]
        found = None
        for block in range(self.right.shape[0]):
            at = slice(block * depth, (block + 1) * depth)
            mine = dot_nn(self.left[chip, :, at], self.right[block, :, columns])
            theirs = dot_nn(self.left_other[chip, :, at], self.right_other[block, :, columns])
            found = mine + theirs if found is None else found + mine + theirs
        return found


class Piece:
    def __init__(self, pair, columns, kind, buffers, sems, result):
        self.pair = pair
        self.place = pair.place
        self.columns = columns
        self.kind = kind
        self.send1, self.recv1, self.send2, self.recv2 = buffers[:4]
        mine = self.recv1.at[0, pair.place.inner if kind == 0 else pair.place.outer]
        self.line = [mine] + list(buffers[4:])
        self.send_sems, self.recv_sems = sems
        self.result = result
        self.sent = []

    def send(self, source, target, slot, far_slot, dp, span=None):
        copy = remote(
            source,
            target,
            self.send_sems.at[slot],
            self.recv_sems.at[far_slot],
            (dp, self.place.span if span is None else span),
        )
        copy.start()
        self.sent.append(copy)

    def arrived(self, target, slot):
        remote(
            target, target, self.send_sems.at[slot], self.recv_sems.at[slot], (self.place.dp, self.place.span)
        ).wait_recv()

    def across(self):
        place = self.place
        return place.at(1 - place.outer, place.inner, place.core)

    def beside(self, offset):
        place = self.place
        return place.at(place.outer, place.inner_plus(offset), place.core)

    def product(self, outer, inner):
        return self.pair.product(outer, inner, self.columns)

    def first(self):
        place, count = self.place, self.place.inner_count
        if self.kind == 0:
            for inner in range(count):
                self.send1[0, inner] = self.product(1 - place.outer, inner).astype(BF)
            self.send(self.send1.at[0], self.recv1.at[0], 0, 0, self.across())
            return
        for offset in range(1, count):
            for outer in range(2):
                self.send1[offset - 1, outer] = self.product(
                    outer, place.inner_plus(offset)
                ).astype(BF)
            self.send(
                self.send1.at[offset - 1],
                self.recv1.at[count - offset - 1],
                offset - 1,
                count - offset - 1,
                self.beside(offset),
            )

    def second(self):
        place, count = self.place, self.place.inner_count
        base = count
        if self.kind == 0:
            self.arrived(self.recv1.at[0], 0)
            for offset in range(1, count):
                inner = place.inner_plus(offset)
                total = self.product(place.outer, inner) + self.recv1[0, inner].astype(F32)
                self.send2[offset - 1] = total.astype(BF)
                self.send(
                    self.send2.at[offset - 1],
                    self.recv2.at[count - offset - 1],
                    base + offset - 1,
                    base + count - offset - 1,
                    self.beside(offset),
                )
            return
        total = self.product(1 - place.outer, place.inner)
        for offset in range(1, count):
            self.arrived(self.recv1.at[offset - 1], offset - 1)
            total = total + self.recv1[offset - 1, 1 - place.outer].astype(F32)
        self.send2[0] = total.astype(BF)
        self.send(self.send2.at[0], self.recv2.at[0], base, base, self.across())

    def total(self):
        place, count = self.place, self.place.inner_count
        base = count
        total = self.product(place.outer, place.inner)
        if self.kind == 0:
            total = total + self.recv1[0, place.inner].astype(F32)
            for offset in range(1, count):
                self.arrived(self.recv2.at[offset - 1], base + offset - 1)
                total = total + self.recv2[offset - 1].astype(F32)
            return total
        for offset in range(1, count):
            total = total + self.recv1[offset - 1, place.outer].astype(F32)
        self.arrived(self.recv2.at[0], base)
        return total + self.recv2[0].astype(F32)


    def shape_of_line(self):
        place = self.place
        half = place.span_count // 2
        low = place.span < half
        depth = jnp.where(low, place.span, place.span_count - 1 - place.span)
        inward = jnp.where(low, place.span + 1, place.span - 1)
        outward = jnp.where(low, place.span - 1, place.span + 1)
        outward = jnp.clip(outward, 0, place.span_count - 1)
        return half, depth, inward, outward

    def line_copy(self, source, target, slot, span):
        base = 2 * self.place.inner_count
        return remote(
            source,
            target,
            self.send_sems.at[base + slot],
            self.recv_sems.at[base + slot],
            (self.place.dp, span),
        )

    def send_inward(self):
        half, depth, inward, outward = self.shape_of_line()
        sum_here, from_out, from_mid = self.line

        @pl.when(depth == half - 1)
        def cross():
            self.line_copy(sum_here, from_mid, 1, inward).start()

        @pl.when(depth < half - 1)
        def in_():
            self.line_copy(sum_here, from_out, 0, inward).start()

    def line_start(self):
        half, depth, inward, outward = self.shape_of_line()
        sum_here, from_out, from_mid = self.line
        sum_here[...] = self.total().astype(BF)

        @pl.when(depth == 0)
        def go():
            self.send_inward()

    def line_in(self):
        half, depth, inward, outward = self.shape_of_line()
        sum_here, from_out, from_mid = self.line

        @pl.when(depth > 0)
        def go():
            self.line_copy(from_out, from_out, 0, outward).wait_recv()
            sum_here[...] = (sum_here[...].astype(F32) + from_out[...].astype(F32)).astype(BF)
            self.send_inward()

    def line_mid(self):
        half, depth, inward, outward = self.shape_of_line()
        sum_here, from_out, from_mid = self.line

        @pl.when(depth == half - 1)
        def go():
            self.line_copy(from_mid, from_mid, 1, inward).wait_recv()
            self.result[...] = (
                sum_here[...].astype(F32) + from_mid[...].astype(F32)
            ).astype(BF)

            @pl.when(depth > 0)
            def out():
                self.line_copy(self.result, self.result, 2, outward).start()

    def line_out(self):
        half, depth, inward, outward = self.shape_of_line()

        @pl.when(depth < half - 1)
        def go():
            self.line_copy(self.result, self.result, 2, inward).wait_recv()

            @pl.when(depth > 0)
            def out():
                self.line_copy(self.result, self.result, 2, outward).start()

    def line_finish(self):
        half, depth, inward, outward = self.shape_of_line()
        sum_here, from_out, from_mid = self.line

        @pl.when(depth == half - 1)
        def cross():
            self.line_copy(sum_here, from_mid, 1, inward).wait_send()

        @pl.when(depth < half - 1)
        def in_():
            self.line_copy(sum_here, from_out, 0, inward).wait_send()

        @pl.when(depth > 0)
        def out():
            self.line_copy(self.result, self.result, 2, outward).wait_send()


    def spread_start(self, results):
        place = self.place
        base = 2 * place.inner_count
        self.results = results
        results[place.span, :, self.columns] = self.total().astype(BF)
        for offset in range(1, place.span_count):
            peer = lax.rem(place.span + offset, place.span_count)
            block = results.at[place.span, :, self.columns]
            self.send(
                block, block, base + offset, base + place.span_count - offset, place.dp, peer
            )

    def spread_wait(self):
        place = self.place
        base = 2 * place.inner_count
        for offset in range(1, place.span_count):
            peer = lax.rem(place.span + offset, place.span_count)
            self.arrived(self.results.at[peer, :, self.columns], base + offset)

    def finish(self):
        for copy in self.sent:
            copy.wait_send()


def cut_columns(width):
    if width > 4096:
        quarter = width // 4 // 128 * 128
        return [slice(i * quarter, (i + 1) * quarter if i < 3 else width) for i in range(4)]
    half = width // 2 // 128 * 128
    return [slice(0, half), slice(half, width)]


def piece_scratch(inner_count, rows, columns, kind, on_line):
    width = columns.stop - columns.start
    if kind == 0:
        shapes = [(1, inner_count, rows, width)] * 2 + [(inner_count - 1, rows, width)] * 2
    else:
        shapes = [(inner_count - 1, 2, rows, width)] * 2 + [(1, rows, width)] * 2
    if on_line:
        shapes += [(rows, width)] * 2
    return shapes


GATE_UP, DOWN, OUT, QKV = range(4)
WAIT_PAIR, ATTEND, CLOSE, WAIT_GRAD, LEND_MIXED, SEND_BLENDED, WAIT_BLENDED, CHAIN, CHAIN_END = range(9)
ORDER = (
    (WAIT_PAIR, DOWN, 0),
    (Piece.first, DOWN, 0),
    (Piece.first, DOWN, 1),
    (WAIT_PAIR, GATE_UP, 0),
    (Piece.first, GATE_UP, 2),
    (Piece.first, GATE_UP, 3),
    (WAIT_GRAD, None, 0),
    (WAIT_PAIR, OUT, 0),
    (Piece.first, GATE_UP, 0),
    (ATTEND, None, 0),
    (CLOSE, None, 0),
    (SEND_BLENDED, None, 0),
    (Piece.second, DOWN, 0),
    (Piece.second, GATE_UP, 2),
    (Piece.line_start, DOWN, 0),
    (LEND_MIXED, None, 0),
    (Piece.second, DOWN, 1),
    (Piece.second, GATE_UP, 0),
    (Piece.line_start, GATE_UP, 2),
    (Piece.first, OUT, 0),
    (Piece.first, OUT, 1),
    (Piece.line_in, DOWN, 0),
    (Piece.second, GATE_UP, 3),
    (Piece.line_in, GATE_UP, 2),
    (WAIT_PAIR, QKV, 0),
    (Piece.first, GATE_UP, 1),
    (Piece.line_start, GATE_UP, 0),
    (Piece.line_mid, DOWN, 0),
    (Piece.second, OUT, 1),
    (Piece.line_start, DOWN, 1),
    (Piece.second, OUT, 0),
    (Piece.line_in, GATE_UP, 0),
    (Piece.line_start, GATE_UP, 3),
    (Piece.first, QKV, 0),
    (Piece.line_start, OUT, 1),
    (WAIT_BLENDED, None, 0),
    (Piece.line_in, DOWN, 1),
    (Piece.line_mid, GATE_UP, 2),
    (Piece.second, GATE_UP, 1),
    (Piece.second, QKV, 0),
    (Piece.line_start, OUT, 0),
    (Piece.line_out, DOWN, 0),
    (Piece.first, QKV, 1),
    (Piece.line_in, GATE_UP, 3),
    (Piece.line_mid, GATE_UP, 0),
    (CHAIN, None, 0),
    (Piece.line_out, GATE_UP, 2),
    (Piece.spread_start, QKV, 0),
    (Piece.second, QKV, 1),
    (Piece.line_mid, DOWN, 1),
    (Piece.line_in, OUT, 0),
    (Piece.line_mid, GATE_UP, 3),
    (Piece.line_start, GATE_UP, 1),
    (CHAIN, None, 1),
    (Piece.line_in, OUT, 1),
    (Piece.spread_start, QKV, 1),
    (Piece.spread_wait, QKV, 0),
    (Piece.line_mid, OUT, 0),
    (Piece.line_mid, OUT, 1),
    (Piece.line_out, OUT, 1),
    (Piece.line_out, DOWN, 1),
    (Piece.line_in, GATE_UP, 1),
    (Piece.line_out, GATE_UP, 0),
    (Piece.line_out, GATE_UP, 3),
    (CHAIN, None, 2),
    (Piece.line_mid, GATE_UP, 1),
    (CHAIN_END, None, 0),
    (Piece.line_out, GATE_UP, 1),
    (Piece.line_out, OUT, 0),
    (Piece.spread_wait, QKV, 1),
)


def backward_kernel(
    dp_count,
    span_count,
    order,
    gate_up_left,
    gate_up_right,
    down_left,
    down_right,
    out_left,
    out_right,
    qkv_left,
    attended_grad_whole,
    query_whole,
    key_whole,
    value_whole,
    raw_whole,
    lse_whole,
    qkv_whole,
    counts,
    cosine,
    sine,
    gate_up_result,
    down_result,
    out_result,
    qkv_result,
    blended_result,
    normed_result,
    attended_grad,
    query,
    key,
    value,
    raw,
    lse,
    qkv_copy,
    load_sem,
    gate_up_own,
    gate_up_other,
    gate_up_right_own,
    gate_up_right_other,
    down_own,
    down_other,
    down_right_own,
    down_right_other,
    out_own,
    out_other,
    out_right_own,
    out_right_other,
    qkv_own,
    qkv_other,
    mixed_other,
    mixed,
    grad_send,
    grad_all,
    key_sum,
    value_sum,
    key_turned,
    query_sum,
    blended_all,
    chain,
    pair_send,
    pair_recv,
    piece_send,
    piece_recv,
    grad_send_sem,
    grad_recv_sem,
    blended_send_sem,
    blended_recv_sem,
    chain_send,
    chain_recv,
    *piece_buffers,
):
    place = Place(dp_count, span_count)
    span, last = place.span, span_count - 1
    rows, width = attended_grad.shape
    group = width // span_count
    heads = group // HEAD_DIM

    loads = []
    for source, target in (
        (attended_grad_whole, attended_grad),
        (key_whole, key),
        (query_whole, query),
        (value_whole, value),
        (raw_whole, raw),
        (lse_whole, lse),
        (qkv_whole, qkv_copy),
    ):
        loads.append(pltpu.make_async_copy(source, target, load_sem.at[len(loads)]))
        loads[-1].start()
    place.greet_all()
    loads[0].wait()
    for index in range(span_count):
        grad_send[index] = attended_grad[:, index * group : (index + 1) * group]
    grad_exchange = Exchange(place, grad_send, grad_all, grad_send_sem, grad_recv_sem)
    grad_exchange.start()
    pairs = [
        Pair(place, *members, pair_send.at[i], pair_recv.at[i])
        for i, members in enumerate(
            (
                (
                    gate_up_left, gate_up_own, gate_up_other,
                    gate_up_right, gate_up_right_own, gate_up_right_other,
                ),
                (down_left, down_own, down_other, down_right, down_right_own, down_right_other),
                (out_left, out_own, out_other, out_right, out_right_own, out_right_other),
                (qkv_left, qkv_own, qkv_other, mixed, mixed, mixed_other),
            )
        )
    ]
    for which in (OUT, DOWN, GATE_UP):
        pairs[which].lend_left()
        pairs[which].lend_right()
    pairs[QKV].lend_left()

    free = list(piece_buffers)
    pieces = []
    for pair, result, on_line in zip(
        pairs, (gate_up_result, down_result, out_result, qkv_result), (True, True, True, False)
    ):
        members = []
        for i, columns in enumerate(cut_columns(pair.right.shape[2])):
            number = 6 if on_line else 4
            buffers, free = free[:number], free[number:]
            at = len(pieces) * 4 + i
            members.append(
                Piece(
                    pair,
                    columns,
                    i % 2,
                    buffers,
                    (piece_send.at[at], piece_recv.at[at]),
                    result.at[:, columns] if on_line else None,
                )
            )
        pieces.append(members)
    def clear(index, unused):
        key_sum[index] = jnp.zeros((rows, group), F32)
        value_sum[index] = jnp.zeros((rows, group), F32)
        return unused

    lax.fori_loop(0, span_count, clear, 0)

    def clear_chain(index, unused):
        chain[index] = jnp.zeros(chain.shape[1:], BF)
        return unused

    @pl.when(span == 0)
    def nothing_from_below():
        lax.fori_loop(1, span_count + 1, clear_chain, 0)

    @pl.when(span == last)
    def nothing_from_above():
        lax.fori_loop(0, span_count, clear_chain, 0)

    cuts = counts[...]
    bounds = [cuts[i : i + 1, 0:1] for i in range(3)]

    def turned_back(rows_in, position):
        cos_here, sin_here = angles_of(cosine, sine, position, heads)
        low = rows_in.astype(BF).astype(F32)
        return (low * cos_here - swap_halves(low) * sin_here).astype(BF)

    for copy in loads[1:]:
        copy.wait()

    def turn_keys(position, unused):
        key_turned[position] = jnp.transpose(key[position])
        return unused

    lax.fori_loop(0, span_count, turn_keys, 0)

    def attend_back(position, unused):
        query_here = (query[position].astype(F32) * SCALE).astype(BF)
        grad_here = grad_all[slot_with(order, position)]
        query_parts = [head_part(query_here, head) for head in range(heads)]
        grad_parts = [head_part(grad_here, head) for head in range(heads)]
        query_stack = jnp.concatenate(query_parts, axis=0)
        grad_stack = jnp.concatenate(grad_parts, axis=0)
        agreed = jnp.transpose(grad_here.astype(F32) * raw[position])
        logs = jnp.transpose(lse[position])
        query_position = (
            lax.broadcasted_iota(jnp.int32, (1, rows), 1) + position * rows
        ).astype(F32)
        start = jnp.zeros((1, rows), F32)
        for cut in bounds:
            start = jnp.where(query_position >= cut, cut, start)
        query_sum[...] = jnp.zeros((group, rows), F32)

        def block(other, unused):
            key_here, value_here, key_back = key[other], value[other], key_turned[other]
            key_position = (
                lax.broadcasted_iota(jnp.int32, (rows, 1), 0) + other * rows
            ).astype(F32)
            allowed = (key_position <= query_position) & (key_position >= start)
            lows, grads = [], []
            for head in range(heads):
                at = slice(head * HEAD_DIM, (head + 1) * HEAD_DIM)
                scores = dot_nt(key_here, query_parts[head])
                weights = jnp.where(allowed, jnp.exp(scores - logs[head : head + 1]), 0.0)
                weights_grad = dot_nt(value_here, grad_parts[head])
                delta = jnp.sum(agreed[at], axis=0, keepdims=True)
                scores_grad = (weights * (weights_grad - delta)).astype(BF)
                lows.append(weights.astype(BF))
                grads.append(scores_grad)
                query_sum[at, :] += dot_nn(key_back[at], scores_grad)
            key_sum[other] += dot_nn(jnp.concatenate(grads, axis=1), query_stack)
            value_sum[other] += dot_nn(jnp.concatenate(lows, axis=1), grad_stack)
            return unused

        lax.fori_loop(0, position + 1, block, 0)
        mixed[position, :, :group] = turned_back(
            jnp.transpose(query_sum[...]) * SCALE, position
        )
        return unused

    def close(position, unused):
        mixed[position, :, group : 2 * group] = turned_back(key_sum[position], position)
        mixed[position, :, 2 * group :] = (
            BLEND_MIX * value_sum[position].astype(BF).astype(F32)
        ).astype(BF)
        return unused

    blended_send = grad_send
    blended_exchange = Exchange(
        place, blended_send, blended_all, blended_send_sem, blended_recv_sem
    )

    def normed_grad(block):
        return dot_nt(mixed[order[block]], qkv_copy[...])

    def pass_on(block, way):
        return remote(
            chain.at[block + 1 - way],
            chain.at[block + 1 - way],
            chain_send.at[way, block],
            chain_recv.at[way, block],
            (place.dp, jnp.minimum(span + 1, last) if way == 0 else jnp.maximum(span - 1, 0)),
        )

    def chain_step(step):
        up = last + span - step
        down = step - (last - span)

        @pl.when((span <= step) & (up > span))
        def going_up():
            block = jnp.clip(up, 0, last)

            @pl.when(span > 0)
            def more():
                pass_on(block, 0).wait_recv()

            chain[block + 1] = (normed_grad(block) + chain[block + 1].astype(F32)).astype(BF)
            pass_on(block, 0).start()

        @pl.when((down >= 0) & (down < span))
        def going_down():
            block = jnp.clip(down, 0, last)

            @pl.when(span < last)
            def more():
                pass_on(block, 1).wait_recv()

            chain[block] = (normed_grad(block) + chain[block].astype(F32)).astype(BF)
            pass_on(block, 1).start()

    def chain_end():
        @pl.when(span > 0)
        def from_below():
            pass_on(span, 0).wait_recv()

        @pl.when(span < last)
        def from_above():
            pass_on(span, 1).wait_recv()

        normed_result[...] = (
            normed_grad(span) + chain[span + 1].astype(F32) + chain[span].astype(F32)
        )

    def send_blended():
        grad_exchange.finish()
        for index in range(span_count):
            blended_send[index] = value_sum[order[index]].astype(BF)
        blended_exchange.start()

    def keep_blended():
        blended_exchange.wait()
        blended_result[...] = jnp.concatenate(
            [blended_all[i] for i in range(span_count)], axis=1
        )

    single = {
        WAIT_GRAD: grad_exchange.wait,
        CLOSE: lambda: lax.fori_loop(0, span_count, close, 0),
        LEND_MIXED: pairs[3].right_copy.start,
        SEND_BLENDED: send_blended,
        WAIT_BLENDED: keep_blended,
        CHAIN_END: chain_end,
    }
    for action, which, number in ORDER:
        if action in single:
            single[action]()
        elif action == WAIT_PAIR:
            pairs[which].wait()
        elif action == ATTEND:
            lax.fori_loop(0, span_count, attend_back, 0)
        elif action == CHAIN:
            for step in [number] if number < 2 else range(2, last):
                chain_step(step)
        elif action == Piece.spread_start:
            pieces[which][number].spread_start(qkv_result)
        else:
            action(pieces[which][number])

    for pair in pairs:
        pair.finish()
    blended_exchange.finish()
    for which, members in enumerate(pieces):
        for member in members:
            if which != QKV:
                member.line_finish()
            member.finish()
    for step in range(last):
        up = last + span - step
        down_block = step - (last - span)

        @pl.when((span <= step) & (up > span))
        def sent_up():
            pass_on(jnp.clip(up, 0, last), 0).wait_send()

        @pl.when((down_block >= 0) & (down_block < span))
        def sent_down():
            pass_on(jnp.clip(down_block, 0, last), 1).wait_send()


def backward_call(dp_count, span_count, order, factors, others, tables):
    (gate_up_left, gate_up_right, down_left, down_right, out_left, out_right, qkv_left) = factors
    rows, width = others[0].shape
    kept = [pltpu.VMEM(member.shape, member.dtype) for member in others]
    group = width // span_count
    inner_count = dp_count // 4
    dma = pltpu.SemaphoreType.DMA
    by_span = (span_count, rows, group)
    mixed_shape = (span_count, rows, 3 * group)

    def less(left):
        return (left.shape[0],) + left.shape[2:]

    scratch = []
    for left, columns_in, on_line in (
        (gate_up_left, gate_up_right.shape[2], True),
        (down_left, down_right.shape[2], True),
        (out_left, out_right.shape[2], True),
        (qkv_left, 3 * group, False),
    ):
        for i, columns in enumerate(cut_columns(columns_in)):
            scratch += [
                pltpu.VMEM(shape, BF)
                for shape in piece_scratch(inner_count, left.shape[2], columns, i % 2, on_line)
            ]
    slots = 2 * inner_count + max(3, span_count)
    return pl.pallas_call(
        functools.partial(backward_kernel, dp_count, span_count),
        out_shape=(
            jax.ShapeDtypeStruct((gate_up_left.shape[2], gate_up_right.shape[2]), BF),
            jax.ShapeDtypeStruct((down_left.shape[2], down_right.shape[2]), BF),
            jax.ShapeDtypeStruct((out_left.shape[2], out_right.shape[2]), BF),
            jax.ShapeDtypeStruct((span_count, qkv_left.shape[2], 3 * group), BF),
            jax.ShapeDtypeStruct((rows, width), BF),
            jax.ShapeDtypeStruct((rows, width), F32),
        ),
        in_specs=[pl.BlockSpec(memory_space=pltpu.SMEM)]
        + [any_spec()] * (len(factors) + len(others))
        + [full_spec()] * len(tables),
        out_specs=(full_spec(),) * 6,
        scratch_shapes=kept
        + [
            dma((len(others),)),
            pltpu.VMEM(less(gate_up_left), BF),
            pltpu.VMEM(less(gate_up_left), BF),
            pltpu.VMEM(gate_up_right.shape, BF),
            pltpu.VMEM(gate_up_right.shape, BF),
            pltpu.VMEM(less(down_left), BF),
            pltpu.VMEM(less(down_left), BF),
            pltpu.VMEM(down_right.shape, BF),
            pltpu.VMEM(down_right.shape, BF),
            pltpu.VMEM(less(out_left), BF),
            pltpu.VMEM(less(out_left), BF),
            pltpu.VMEM(out_right.shape, BF),
            pltpu.VMEM(out_right.shape, BF),
            pltpu.VMEM(less(qkv_left), BF),
            pltpu.VMEM(less(qkv_left), BF),
            pltpu.VMEM(mixed_shape, BF),
            pltpu.VMEM(mixed_shape, BF),
            pltpu.VMEM(by_span, BF),
            pltpu.VMEM(by_span, BF),
            pltpu.VMEM(by_span, F32),
            pltpu.VMEM(by_span, F32),
            pltpu.VMEM((span_count, group, rows), BF),
            pltpu.VMEM((group, rows), F32),
            pltpu.VMEM(by_span, BF),
            pltpu.VMEM((span_count + 1, rows, width), BF),
            dma((4, 4)),
            dma((4, 4)),
            dma((16, slots)),
            dma((16, slots)),
            dma((span_count,)),
            dma((span_count,)),
            dma((span_count,)),
            dma((span_count,)),
            dma((2, span_count)),
            dma((2, span_count)),
        ]
        + scratch,
        compiler_params=pltpu.CompilerParams(
            collective_id=1, has_side_effects=True, vmem_limit_bytes=61 << 20
        ),
    )(order, *factors, *others, *tables)


def update_rows(master, first_state, second_state, gradient, rate, decay):
    next_first = BETA_FIRST * first_state + (1.0 - BETA_FIRST) * gradient
    next_second = BETA_SECOND * second_state + (1.0 - BETA_SECOND) * gradient * gradient
    first_hat = next_first * (1.0 / (1.0 - BETA_FIRST**STEP))
    second_hat = next_second * (1.0 / (1.0 - BETA_SECOND**STEP))
    new_master = master - rate * (first_hat / (jnp.sqrt(second_hat) + ADAM_EPS) + decay * master)
    return (new_master, next_first, next_second)


def finish_kernel(
    qkv_total,
    out_total,
    gate_up_total,
    down_total,
    gains,
    gains_first,
    gains_second,
    tokens,
    mid_grad,
    normed_grad,
    gains_rows,
    blended_grad,
    layer_low,
    qkv,
    qkv_first,
    qkv_second,
    out,
    out_first,
    out_second,
    gate_up,
    gate_up_first,
    gate_up_second,
    down,
    down_first,
    down_second,
    layer_out,
    tokens_grad,
    values_grad,
    new_gains,
    new_gains_first,
    new_gains_second,
    *rest,
):
    results, held, sums, in_sem, out_sem = rest[:12], rest[12:24], rest[24], rest[25], rest[26]
    states = (
        (qkv, qkv_first, qkv_second),
        (out, out_first, out_second),
        (gate_up, gate_up_first, gate_up_second),
        (down, down_first, down_second),
    )
    width = tokens.shape[1]
    span_count = qkv_total.shape[0]
    group = width // span_count

    def qkv_rows(part):
        def rows(at):
            return jnp.concatenate(
                [
                    qkv_total[i, at, part * group : (part + 1) * group].astype(F32)
                    for i in range(span_count)
                ],
                axis=1,
            )

        return rows

    def rows_of(total, columns):
        return lambda at: total[at, columns].astype(F32)

    parts = []
    for columns in cut_columns(gate_up_total.shape[1]):
        parts.append((2, columns, rows_of(gate_up_total, columns)))
    for part in range(3):
        parts.append((0, slice(part * width, (part + 1) * width), qkv_rows(part)))
    for columns in cut_columns(width):
        parts.append((3, columns, rows_of(down_total, columns)))
    parts.append((1, slice(0, width), rows_of(out_total, slice(0, width))))

    def moves(number, source, target, sems):
        weight, columns, _ = parts[number]
        return [
            pltpu.make_async_copy(
                source[i].at[:, columns], target[i].at[:, columns], sems.at[number, i]
            )
            for i in range(3)
        ]

    loads, stores = [], []
    for number, (weight, _, _) in enumerate(parts):
        here = held[3 * weight : 3 * weight + 3]
        loads.append(moves(number, states[weight], here, in_sem))
        stores.append(moves(number, here, results[3 * weight : 3 * weight + 3], out_sem))
        for copy in loads[-1]:
            copy.start()

    residual = tokens[...].astype(F32)
    scaled, inverse = normalize_parts(residual)
    tokens_grad[...] = mid_grad[...] + norm_backward(
        normed_grad[...], scaled, inverse, gains_rows[0:1, :]
    )
    layer_out[...] = layer_low[...]
    sums[...] = jnp.zeros_like(sums)
    values_grad[...] = (1.0 - BLEND_MIX) * blended_grad[...].astype(F32)

    for number, (weight, columns, total) in enumerate(parts):
        here = held[3 * weight : 3 * weight + 3]
        for copy in loads[number]:
            copy.wait()
        owned = here[0].shape[0]
        wants_sum = weight in (0, 2)

        def step(index, unused):
            at = pl.ds(pl.multiple_of(index * 16, 16), 16)
            gradient = total(at)
            master = here[0][at, columns]
            if wants_sum:
                partial = jnp.sum(
                    gradient * master.astype(BF).astype(F32), axis=1, keepdims=True
                )
                lane = 0 if weight == 0 else 1
                slot = lax.broadcasted_iota(jnp.int32, (16, 128), 1) == lane
                sums[at, :] += jnp.where(slot, partial, 0.0)
            updated = update_rows(
                master,
                here[1][at, columns],
                here[2][at, columns],
                gradient,
                MATRIX_RATE,
                MATRIX_DECAY,
            )
            for i in range(3):
                here[i][at, columns] = updated[i]
            return unused

        lax.fori_loop(0, owned // 16, step, 0)
        for copy in stores[number]:
            copy.start()

    gain = gains[...]
    gains_total = jnp.transpose(sums[...])[:2, :] / gain.astype(BF).astype(F32)
    updated = update_rows(gain, gains_first[...], gains_second[...], gains_total, GAIN_RATE, 0.0)
    new_gains[...], new_gains_first[...], new_gains_second[...] = updated
    for group_of_copies in stores:
        for copy in group_of_copies:
            copy.wait()


def finish_call(totals, gains_states, token_parts, states):
    flat = [member for weight in states for member in weight]
    rows, width = token_parts[0].shape
    gains_shape = jax.ShapeDtypeStruct(gains_states[0].shape, F32)
    dma = pltpu.SemaphoreType.DMA
    count = len(cut_columns(totals[2].shape[1])) + 3 + 2 + 1
    return pl.pallas_call(
        finish_kernel,
        out_shape=(
            jax.ShapeDtypeStruct((rows, width), BF),
            jax.ShapeDtypeStruct((rows, width), F32),
            jax.ShapeDtypeStruct((rows, width), F32),
            gains_shape,
            gains_shape,
            gains_shape,
        )
        + tuple(jax.ShapeDtypeStruct(member.shape, F32) for member in flat),
        in_specs=[full_spec()] * 13 + [any_spec()] * 12,
        out_specs=(full_spec(),) * 6 + (any_spec(),) * 12,
        scratch_shapes=[pltpu.VMEM(member.shape, F32) for member in flat]
        + [
            pltpu.VMEM((gains_states[0].shape[1], 128), F32),
            dma((count, 3)),
            dma((count, 3)),
        ],
        compiler_params=pltpu.CompilerParams(vmem_limit_bytes=VMEM_BYTES),
    )(*totals, *gains_states, *token_parts, *flat)


def to_heads(rows, span_count):
    return lax.all_to_all(
        rows.reshape(rows.shape[0], span_count, rows.shape[1] // span_count),
        "seq",
        split_axis=1,
        concat_axis=0,
        tiled=True,
    ).reshape(rows.shape[0] * span_count, rows.shape[1] // span_count)


def to_spans(columns, span_count):
    rows_here = columns.shape[0] // span_count
    got = lax.all_to_all(
        columns.reshape(span_count, rows_here, columns.shape[1]),
        "seq",
        split_axis=0,
        concat_axis=0,
        tiled=True,
    )
    return jnp.transpose(got, (1, 0, 2)).reshape(rows_here, columns.shape[1] * span_count)


def on_device(
    tokens,
    first_values,
    out_grad,
    segments,
    span_order,
    qkv_weight,
    out_weight,
    gate_up_weight,
    down_weight,
    norm_gains,
    first_qkv,
    first_out,
    first_gate_up,
    first_down,
    first_gains,
    second_qkv,
    second_out,
    second_gate_up,
    second_down,
    second_gains,
):
    span_count = lax.axis_size("seq")
    mine = lax.axis_index("seq")
    owned_rows, triple = qkv_weight.shape
    model_width = triple // 3
    group = model_width // span_count
    group_heads = group // HEAD_DIM
    residual = tokens[0].astype(F32)
    rows_here = residual.shape[0]
    length = rows_here * span_count
    hidden_width = gate_up_weight.shape[1] // 2

    dp_count = lax.axis_size("dp")
    gains_owned = norm_gains.astype(BF).astype(F32)
    in_kernels = (
        length * model_width <= 1 << 20
        and dp_count % 4 == 0
        and dp_count >= 8
        and span_count % 2 == 0
        and group % 128 == 0
        and span_count * HEAD_DIM // 2 <= 128
        and hidden_width % 256 == 0
    )
    if in_kernels:
        half_width = HEAD_DIM // 2
        lane = lax.broadcasted_iota(jnp.int32, (rows_here, 128), 1)
        position = lax.broadcasted_iota(jnp.int32, (rows_here, 128), 0) + lane // half_width * rows_here
        frequency = jnp.exp(
            (jnp.arange(128, dtype=jnp.int32) % half_width).astype(F32)
            * (-math.log(ROPE_BASE) / half_width)
        )
        angles = lax.optimization_barrier(position).astype(F32) * frequency[None, :]
        cosine, sine = jnp.cos(angles), jnp.sin(angles)
        gains_states = tuple(
            jnp.transpose(member) for member in (norm_gains, first_gains, second_gains)
        )
        (
            counts, gains_rows, layer_low, hidden_mid_grad, mid_grad_low, normed_mid_left,
            attended_left, attended_grad, qkv_copy, normed_left, query_pos, key_pos, value_pos,
            raw_pos, lse_pos, gate_up_grad, activation_left,
        ) = forward_call(
            dp_count, span_count, span_order, tokens[0], first_values[0], segments,
            gains_states[0], qkv_weight, out_weight, gate_up_weight, down_weight, cosine, sine, out_grad[0],
        )
        def in_blocks(left):
            return left.reshape(dp_count // 2, 2, left.shape[0] // dp_count, left.shape[1])

        factors = (
            in_blocks(normed_mid_left),
            gate_up_grad[None],
            in_blocks(activation_left),
            out_grad,
            in_blocks(attended_left),
            mid_grad_low[None],
            in_blocks(normed_left),
        )
        others = (
            attended_grad,
            query_pos, key_pos, value_pos, raw_pos, lse_pos, qkv_copy,
        )
        gate_up_total, down_total, out_total, qkv_part, blended_grad, normed_in_grad = backward_call(
            dp_count, span_count, span_order, factors, others, (counts, cosine, sine)
        )
        finished = finish_call(
            (qkv_part, out_total, gate_up_total, down_total),
            gains_states,
            (tokens[0], hidden_mid_grad, normed_in_grad, gains_rows, blended_grad, layer_low),
            (
                (qkv_weight, first_qkv, second_qkv),
                (out_weight, first_out, second_out),
                (gate_up_weight, first_gate_up, second_gate_up),
                (down_weight, first_down, second_down),
            ),
        )
        new_gains = tuple(jnp.transpose(member) for member in finished[3:6])
        return (
            tuple(member[None] for member in finished[:3])
            + finished[6::3]
            + new_gains[:1]
            + finished[7::3]
            + new_gains[1:2]
            + finished[8::3]
            + new_gains[2:]
        )

    qkv_owned = qkv_weight.reshape(owned_rows, 3, model_width).astype(BF)
    qkv_mine = lax.dynamic_slice_in_dim(qkv_owned, mine * group, group, 2).reshape(
        owned_rows, 3 * group
    )
    gains_full = lax.all_gather(norm_gains.astype(BF), "dp", axis=0, tiled=True).astype(F32)
    qkv_copy = lax.all_gather(qkv_mine, "dp", axis=0, tiled=True)
    out_copy = lax.all_gather(out_weight.astype(BF), "dp", axis=0, tiled=True)
    gate_up_copy = lax.all_gather(gate_up_weight.astype(BF), "dp", axis=0, tiled=True)
    down_copy = lax.all_gather(down_weight.astype(BF), "dp", axis=0, tiled=True)

    row_index = jnp.arange(length, dtype=jnp.int32)
    owner_table = (row_index // rows_here)[:, None] == jnp.arange(span_count, dtype=jnp.int32)[
        None, :
    ]
    positions = (
        jnp.sum(jnp.where(owner_table, span_order[None, :], 0), axis=1) * rows_here
        + row_index % rows_here
    )
    all_segments = lax.all_gather(segments[0], "seq", axis=0, tiled=True)
    cosine, sine_table = rotary(positions)
    allowed = (all_segments[:, None] == all_segments[None, :]) & (
        positions[None, :] <= positions[:, None]
    )

    scaled_in, inverse_in = normalize_parts(residual)
    normed_in = (scaled_in * gains_full[:, 0]).astype(BF)
    normed_all = lax.all_gather(normed_in, "seq", axis=0, tiled=True)
    first_all = to_heads(first_values[0], span_count)
    mixed = dot_nn(normed_all, qkv_copy)
    queries = rotate(
        mixed[:, :group].reshape(length, group_heads, HEAD_DIM), cosine, sine_table
    ).astype(BF)
    keys = rotate(
        mixed[:, group : 2 * group].reshape(length, group_heads, HEAD_DIM), cosine, sine_table
    ).astype(BF)
    blended = (
        (BLEND_MIX * mixed[:, 2 * group :] + (1.0 - BLEND_MIX) * first_all.astype(F32))
        .astype(BF)
        .reshape(length, group_heads, HEAD_DIM)
    )
    scores = jnp.einsum("qhd,khd->hqk", queries, keys, preferred_element_type=F32) * SCALE
    masked = jnp.where(allowed[None], scores, MASK_FILL)
    highest = jnp.max(masked, axis=-1, keepdims=True)
    raised = jnp.where(allowed[None], jnp.exp(masked - highest), 0.0)
    weights = raised / jnp.sum(raised, axis=-1, keepdims=True)
    weights_low = weights.astype(BF)
    attended_raw = jnp.einsum("hqk,khd->qhd", weights_low, blended, preferred_element_type=F32)
    attended = to_spans(attended_raw.reshape(length, group).astype(BF), span_count)

    hidden_mid = residual + dot_nn(attended, out_copy)
    scaled_mid, inverse_mid = normalize_parts(hidden_mid)
    normed_mid = (scaled_mid * gains_full[:, 1]).astype(BF)
    gate_up = dot_nn(normed_mid, gate_up_copy)
    gate_part = gate_up[:, :hidden_width]
    upward = gate_up[:, hidden_width:]
    sigmoid_gate = jax.nn.sigmoid(gate_part)
    swish_gate = gate_part * sigmoid_gate
    activation = (swish_gate * upward).astype(BF)
    layer_out = (hidden_mid + dot_nn(activation, down_copy)).astype(BF)
    back_rows = out_grad[0]
    activation_grad = dot_nt(back_rows, down_copy)
    gate_up_grad = jnp.concatenate(
        [
            activation_grad * upward * sigmoid_gate * (1.0 + gate_part * (1.0 - sigmoid_gate)),
            activation_grad * swish_gate,
        ],
        axis=1,
    ).astype(BF)
    normed_mid_grad = dot_nt(gate_up_grad, gate_up_copy)
    hidden_mid_grad = back_rows.astype(F32) + norm_backward(
        normed_mid_grad, scaled_mid, inverse_mid, gains_full[:, 1]
    )
    mid_grad_low = hidden_mid_grad.astype(BF)
    attended_grad = to_heads(dot_nt(mid_grad_low, out_copy).astype(BF), span_count)

    heads_grad = attended_grad.reshape(length, group_heads, HEAD_DIM)
    delta = jnp.transpose(jnp.sum(heads_grad.astype(F32) * attended_raw, axis=-1))
    weights_grad = jnp.einsum("qhd,khd->hqk", heads_grad, blended, preferred_element_type=F32)
    scores_grad = (weights * (weights_grad - delta[..., None])).astype(BF)
    queries_grad = (
        jnp.einsum("hqk,khd->qhd", scores_grad, keys, preferred_element_type=F32) * SCALE
    ).astype(BF).astype(F32)
    keys_grad = (
        jnp.einsum("hqk,qhd->khd", scores_grad, queries, preferred_element_type=F32) * SCALE
    ).astype(BF).astype(F32)
    blended_grad = jnp.einsum(
        "hqk,qhd->khd", weights_low, heads_grad, preferred_element_type=F32
    ).astype(BF).reshape(length, group)
    values_grad = (1.0 - BLEND_MIX) * to_spans(blended_grad, span_count).astype(F32)
    mixed_grad = jnp.concatenate(
        [
            rotate(queries_grad, cosine, -sine_table).reshape(length, group),
            rotate(keys_grad, cosine, -sine_table).reshape(length, group),
            BLEND_MIX * blended_grad.astype(F32),
        ],
        axis=1,
    ).astype(BF)
    normed_in_grad = lax.psum_scatter(
        dot_nt(mixed_grad, qkv_copy).astype(BF), "seq", scatter_dimension=0, tiled=True
    ).astype(F32)
    tokens_grad = hidden_mid_grad + norm_backward(
        normed_in_grad, scaled_in, inverse_in, gains_full[:, 0]
    )

    def to_owner(terms):
        return lax.psum_scatter(terms.astype(BF), "dp", scatter_dimension=0, tiled=True)

    qkv_part = lax.all_gather(to_owner(dot_tn(normed_all, mixed_grad)), "seq", axis=0)
    qkv_total = (
        jnp.transpose(qkv_part.reshape(span_count, owned_rows, 3, group), (1, 2, 0, 3))
        .reshape(owned_rows, triple)
        .astype(F32)
    )
    out_total, gate_up_total, down_total = lax.psum(
        (
            to_owner(dot_tn(attended, mid_grad_low)),
            to_owner(dot_tn(normed_mid, gate_up_grad)),
            to_owner(dot_tn(activation, back_rows)),
        ),
        "seq",
    )
    out_total, gate_up_total, down_total = (
        out_total.astype(F32),
        gate_up_total.astype(F32),
        down_total.astype(F32),
    )

    gains_total = jnp.stack(
        [
            jnp.sum(qkv_total * qkv_weight.astype(BF).astype(F32), axis=1),
            jnp.sum(gate_up_total * gate_up_weight.astype(BF).astype(F32), axis=1),
        ],
        axis=1,
    ) / gains_owned
    masters = (qkv_weight, out_weight, gate_up_weight, down_weight, norm_gains)
    firsts = (first_qkv, first_out, first_gate_up, first_down, first_gains)
    seconds = (second_qkv, second_out, second_gate_up, second_down, second_gains)
    totals = (qkv_total, out_total, gate_up_total, down_total, gains_total)
    rate_list = (MATRIX_RATE, MATRIX_RATE, MATRIX_RATE, MATRIX_RATE, GAIN_RATE)
    decays = (MATRIX_DECAY, MATRIX_DECAY, MATRIX_DECAY, MATRIX_DECAY, 0.0)
    updated = [
        apply_adamw(masters[i], firsts[i], seconds[i], totals[i], rate_list[i], decays[i])
        for i in range(5)
    ]
    return (
        (layer_out[None], tokens_grad[None], values_grad[None])
        + tuple(member[0] for member in updated)
        + tuple(member[1] for member in updated)
        + tuple(member[2] for member in updated)
    )


def solution(mesh):
    rows = P("dp", "seq", None)
    owned = P("dp", None)
    return jax.shard_map(
        on_device,
        mesh=mesh,
        in_specs=(rows, rows, rows, P("dp", "seq"), P()) + (owned,) * 15,
        out_specs=(rows,) * 3 + (owned,) * 15,
        check_vma=False,
    )
```

profile of v0, /device:TPU:0, one launch (start us, length us, event | category | flops | bytes accessed | tf_op | source)
XLA Modules:
  0.0 295.1 jit_solution(16791625706844842832)
XLA Ops:
  0.7 1.2 fusion
  1.9 116.0 %shard_map.331 = (f32[8,128]{1,0:T(8,128)}, f32[8,1024]{1,0:T(8,128)}, bf16[256,1024]{1,0:T(8,128)(2,1)}, f32[256,1024]{1,0:T(8,128)}, bf16[256,1024]{1,0:T(8,12...) custom-call(s32[4]{0:T(128)} %order.3, ...), custom_call_target="tpu_custom_call" | custom-call | tf_op jit(solution)/shard_map/pallas_call | solution.py:823
  117.9 158.7 %shard_map.332 = (bf16[128,5632]{1,0:T(8,128)(2,1)}, bf16[352,1024]{1,0:T(8,128)(2,1)}, bf16[128,1024]{1,0:T(8,128)(2,1)}, bf16[4,128,768]{2,1,0:T(8,128)(2,1)},...) custom-call(s32[4]{0:T(128)} %order.3, bf16[4,2,128,256]{3,2,1,0:T(8,128)(2,1)} %bitcast.26, ...), custom_call_target="tpu_custom_call" | custom-call | tf_op jit(solution)/shard_map/pallas_call | solution.py:1623
  276.7 18.3 %shard_map.333 = (bf16[256,1024]{1,0:T(8,128)(2,1)}, f32[256,1024]{1,0:T(8,128)}, f32[256,1024]{1,0:T(8,128)}, f32[2,128]{1,0:T(2,128)}, f32[2,128]{1,0:T(2,128)...) custom-call(bf16[4,128,768]{2,1,0:T(8,128)(2,1)} %get-tuple-element., ...), custom_call_target="tpu_custom_call" | custom-call | tf_op jit(solution)/shard_map/pallas_call | solution.py:1835
  (4 shorter events, 0.0 us)
where the time goes:
time: 296 us; the launch traced here: 295 us
  Pallas kernels  293 us (99%)
    pallas_call x1, Pallas kernels, backward_call(): pl.pallas_call(functools.partial(backward_kernel, dp_count, span_count),...  159 us
    pallas_call x1, Pallas kernels, forward_call(): pl.pallas_call(functools.partial(forward_kernel, dp_count, span_count), o...  116 us
    pallas_call x1, Pallas kernels, finish_call(): pl.pallas_call(finish_kernel, out_shape=(jax.ShapeDtypeStruct((rows, widt...  18.3 us

commit v1 on v0

--- a/solution.py
+++ b/solution.py
@@ -1490,6 +1490,15 @@
     def normed_grad(block):
         return dot_nt(mixed[order[block]], qkv_copy[...])
 
+    def add_normed(block, at):
+        def step(index, unused):
+            here = pl.ds(pl.multiple_of(index * 256, 256), 256)
+            more = dot_nt(mixed[order[block]], qkv_copy[here, :])
+            chain[at, :, here] = (more + chain[at, :, here].astype(F32)).astype(BF)
+            return unused
+
+        lax.fori_loop(0, width // 256, step, 0)
+
     def pass_on(block, way):
         return remote(
             chain.at[block + 1 - way],
@@ -1511,7 +1520,7 @@
             def more():
                 pass_on(block, 0).wait_recv()
 
-            chain[block + 1] = (normed_grad(block) + chain[block + 1].astype(F32)).astype(BF)
+            add_normed(block, block + 1)
             pass_on(block, 0).start()
 
         @pl.when((down >= 0) & (down < span))
@@ -1522,7 +1531,7 @@
             def more():
                 pass_on(block, 1).wait_recv()
 
-            chain[block] = (normed_grad(block) + chain[block].astype(F32)).astype(BF)
+            add_normed(block, block)
             pass_on(block, 1).start()
 
     def chain_end():

time: 296 us -> 297 us (level)
  no operation moved by 1% of the time
where the time goes in v1:
time: 297 us; the launch traced here: 296 us
  Pallas kernels  294 us (99%)
    pallas_call x1, Pallas kernels, backward_call(): pl.pallas_call(functools.partial(backward_kernel, dp_count, span_count),...  159 us
    pallas_call x1, Pallas kernels, forward_call(): pl.pallas_call(functools.partial(forward_kernel, dp_count, span_count), o...  116 us
    pallas_call x1, Pallas kernels, finish_call(): pl.pallas_call(finish_kernel, out_shape=(jax.ShapeDtypeStruct((rows, widt...  18.3 us

profile of v1, /device:TPU:0, one launch (start us, length us, event | category | flops | bytes accessed | tf_op | source)
XLA Modules:
  0.0 295.7 jit_solution(13248225656585336652)
XLA Ops:
  0.7 1.2 fusion
  1.9 116.0 %shard_map.331 = (f32[8,128]{1,0:T(8,128)}, f32[8,1024]{1,0:T(8,128)}, bf16[256,1024]{1,0:T(8,128)(2,1)}, f32[256,1024]{1,0:T(8,128)}, bf16[256,1024]{1,0:T(8,12...) custom-call(s32[4]{0:T(128)} %order.3, ...), custom_call_target="tpu_custom_call" | custom-call | tf_op jit(solution)/shard_map/pallas_call | solution.py:823
  117.9 159.4 %shard_map.332 = (bf16[128,5632]{1,0:T(8,128)(2,1)}, bf16[352,1024]{1,0:T(8,128)(2,1)}, bf16[128,1024]{1,0:T(8,128)(2,1)}, bf16[4,128,768]{2,1,0:T(8,128)(2,1)},...) custom-call(s32[4]{0:T(128)} %order.3, bf16[4,2,128,256]{3,2,1,0:T(8,128)(2,1)} %bitcast.26, ...), custom_call_target="tpu_custom_call" | custom-call | tf_op jit(solution)/shard_map/pallas_call | solution.py:1632
  277.3 18.3 %shard_map.333 = (bf16[256,1024]{1,0:T(8,128)(2,1)}, f32[256,1024]{1,0:T(8,128)}, f32[256,1024]{1,0:T(8,128)}, f32[2,128]{1,0:T(2,128)}, f32[2,128]{1,0:T(2,128)...) custom-call(bf16[4,128,768]{2,1,0:T(8,128)(2,1)} %get-tuple-element., ...), custom_call_target="tpu_custom_call" | custom-call | tf_op jit(solution)/shard_map/pallas_call | solution.py:1844
  (4 shorter events, 0.0 us)
